TPU v7x, 32 devices: a whole 2x2x4 slice. The times are simulated.
32 devices in a mesh: ctx: 2 (over core), exp: 4 (over y, x), req: 4 (over z).
Axes of the slice: x: 2, y: 2, z: 4, core: 2. Of those that a mesh axis runs over, the one named last changes fastest.
Arguments:
- queries: bfloat16 [64, 2, 128, 576], P('req', None, ('ctx', 'exp')), parts along dimension 0, may hold values from -21 to 21
- latent_cache: bfloat16 [64, 4096, 576], P('req', ('ctx', 'exp')), parts along dimension 0, may hold values from -4 to 4
- context_lengths: int32 [64], P('req'), parts along dimension 0, may hold values from 16 to 4095, as said below
- value_up: bfloat16 [128, 512, 128], P(('ctx', 'exp')), may hold values from -0.25 to 0.25
- out_proj: bfloat16 [16384, 7168], P(('ctx', 'exp')), may hold values from -0.09375 to 0.09375
- residual: bfloat16 [128, 7168], P(('req', 'exp')), parts along dimension 0, may hold values from -3 to 3
- norm_gain: bfloat16 [7168], replicated, may hold values from 0.099609375 to 1.8984375
- router: bfloat16 [7168, 4], replicated, may hold values from -0.125 to 0.125
- routes: int32 [128, 2], P(('req', 'exp')), parts along dimension 0, may hold values from 0 to 3, all different within a row; in each aligned block of 8 rows (0 to 7, 8 to 15, ...) at most 4 rows name the same one
- expert_gate: bfloat16 [4, 7168, 1024], P('exp', None, 'ctx'), may hold values from -0.0625 to 0.0625
- expert_up: bfloat16 [4, 7168, 1024], P('exp', None, 'ctx'), may hold values from -0.0625 to 0.0625
- expert_down: bfloat16 [4, 1024, 7168], P('exp', 'ctx'), may hold values from -0.375 to 0.375
Outputs:
- output: bfloat16 [128, 7168], P(('req', 'exp'), 'ctx'), parts along dimension 0
There are 4 independent parts, one for each index of `req`. A program takes and returns all parts, laid end to end along the dimension named above; an argument that names none is the same for every part. Nothing has to cross between parts.
Inputs may be any that keep to these rules, and one draw needn't show every extreme that they name: Verify row j of request r sees context positions below context_lengths[r] + j; in every draw one request has 4095. `routes`: each row names 2 different experts; in each aligned block of 8 rows (the rows of one index of exp) no expert is named by more than 4 rows.
All inputs are finite; a program needn't handle non-finite values.
Results may differ from a plain program's by a relative error of at most 0.028.
Values may be sent and summed in bfloat16 or wider, within the bound.
A program may use at most 128 MiB of HBM per device.

v0:
```python
import math

import jax
import jax.numpy as jnp
from jax import lax
from jax.sharding import PartitionSpec as P

route_scale = 2.5


def on_device(
    queries,
    latent_cache,
    context_lengths,
    value_up,
    out_proj,
    residual,
    norm_gain,
    router,
    routes,
    expert_gate,
    expert_up,
    expert_down,
):
    latent_width = value_up.shape[1]
    value_width = value_up.shape[2]
    rope_width = queries.shape[3] - latent_width
    score_scale = 1.0 / math.sqrt(value_width + rope_width)
    heads_here = queries.shape[2]
    block_len = latent_cache.shape[1]
    device = lax.axis_index(("ctx", "exp"))
    all_queries = lax.all_gather(queries, ("ctx", "exp"), axis=2, tiled=True)
    scores = (
        jnp.einsum("rjhd,rtd->rjht", all_queries, latent_cache, preferred_element_type=jnp.float32)
        * score_scale
    )
    positions = device * block_len + jnp.arange(block_len, dtype=jnp.int32)
    visible_upto = context_lengths[:, None] + jnp.arange(2, dtype=jnp.int32)[None, :]
    visible = positions[None, None, None, :] < visible_upto[:, :, None, None]
    masked = jnp.where(visible, scores, -1e30)
    row_max = lax.pmax(jnp.max(masked, axis=-1), ("ctx", "exp"))
    weights = jnp.where(visible, jnp.exp(masked - row_max[..., None]), 0.0)
    weight_sum = jnp.sum(weights, axis=-1)
    latents = latent_cache[:, :, :latent_width]
    weighted = jnp.einsum(
        "rjht,rtl->rjhl", weights.astype(jnp.bfloat16), latents, preferred_element_type=jnp.float32
    )
    summed, sum_all = lax.psum((weighted, weight_sum), ("ctx", "exp"))
    own_weighted = lax.dynamic_slice_in_dim(summed, device * heads_here, heads_here, 2)
    own_sum = lax.dynamic_slice_in_dim(sum_all, device * heads_here, heads_here, 2)
    context = (own_weighted / own_sum[..., None]).astype(jnp.bfloat16)
    head_out = jnp.einsum(
        "rjhl,hlv->rjhv", context, value_up, preferred_element_type=jnp.float32
    ).astype(jnp.bfloat16)
    row_total = head_out.shape[0] * head_out.shape[1]
    head_out = head_out.reshape(row_total, heads_here * value_width)
    own_rows = residual.shape[0]
    owner_index = lax.axis_index("exp")
    attention_all = lax.psum(
        jnp.dot(head_out, out_proj, preferred_element_type=jnp.float32), ("ctx", "exp")
    )
    attention = lax.dynamic_slice_in_dim(attention_all, owner_index * own_rows, own_rows, 0)
    hidden = (residual.astype(jnp.float32) + attention).astype(jnp.bfloat16)
    hidden_wide = hidden.astype(jnp.float32)
    inverse = lax.rsqrt(jnp.mean(hidden_wide * hidden_wide, axis=-1, keepdims=True) + 1e-06)
    normed = (hidden_wide * inverse * norm_gain.astype(jnp.float32)).astype(jnp.bfloat16)
    affinity = jax.nn.sigmoid(jnp.dot(normed, router, preferred_element_type=jnp.float32))
    expert_count = router.shape[1]
    top_count = routes.shape[1]
    capacity = max(2, own_rows * top_count // expert_count)
    chosen = (
        routes[:, :, None] == jnp.arange(expert_count, dtype=jnp.int32)[None, None, :]
    ).astype(jnp.float32)
    picked = jnp.sum(chosen * affinity[:, None, :], axis=-1)
    gate_weights = route_scale * picked / jnp.sum(picked, axis=-1, keepdims=True)
    per_row = jnp.sum(chosen, axis=1)
    earlier = jnp.cumsum(per_row, axis=0) - per_row
    slot_index = jnp.sum(chosen * earlier[:, None, :], axis=-1)
    slot_hot = (
        slot_index[:, :, None] == jnp.arange(capacity, dtype=jnp.float32)[None, None, :]
    ).astype(jnp.float32)
    placement = chosen[:, :, :, None] * slot_hot[:, :, None, :]
    row_place = jnp.sum(placement, axis=1).reshape(own_rows, expert_count * capacity)
    gate_place = jnp.sum(placement * gate_weights[:, :, None, None], axis=1).reshape(
        own_rows, expert_count * capacity
    )
    model_width = normed.shape[1]
    outgoing = jnp.einsum(
        "rs,rd->sd", row_place.astype(jnp.bfloat16), normed, preferred_element_type=jnp.float32
    ).astype(jnp.bfloat16)
    outgoing = outgoing.reshape(expert_count, capacity, model_width)
    arrived = lax.all_to_all(outgoing, "exp", split_axis=0, concat_axis=0, tiled=True)
    gate_part = jnp.einsum(
        "scd,df->scf", arrived, expert_gate[0], preferred_element_type=jnp.float32
    )
    up_part = jnp.einsum("scd,df->scf", arrived, expert_up[0], preferred_element_type=jnp.float32)
    active = (jax.nn.silu(gate_part) * up_part).astype(jnp.bfloat16)
    partial_out = jnp.einsum(
        "scf,fd->scd", active, expert_down[0], preferred_element_type=jnp.float32
    )
    col_width = model_width // lax.axis_size("ctx")
    ctx_index = lax.axis_index("ctx")
    own_cols = lax.dynamic_slice_in_dim(hidden_wide, ctx_index * col_width, col_width, 1)
    full_sum = lax.psum(partial_out.astype(jnp.bfloat16), "ctx").astype(jnp.float32)
    returned = lax.all_to_all(
        full_sum.astype(jnp.bfloat16), "exp", split_axis=0, concat_axis=0, tiled=True
    ).astype(full_sum.dtype)
    returned = lax.dynamic_slice_in_dim(returned, ctx_index * col_width, col_width, 2)
    mixture = jnp.dot(
        gate_place,
        returned.reshape(expert_count * capacity, col_width),
        precision=lax.Precision.HIGHEST,
    )
    return (own_cols + mixture).astype(jnp.bfloat16)


def solution(mesh):
    return jax.shard_map(
        on_device,
        mesh=mesh,
        in_specs=(
            P("req", None, ("ctx", "exp"), None),
            P("req", ("ctx", "exp"), None),
            P("req"),
            P(("ctx", "exp"), None, None),
            P(("ctx", "exp"), None),
            P(("req", "exp"), None),
            P(),
            P(),
            P(("req", "exp"), None),
            P("exp", None, "ctx"),
            P("exp", None, "ctx"),
            P("exp", "ctx", None),
        ),
        out_specs=P(("req", "exp"), "ctx"),
        check_vma=False,
    )
```

profile of v0, /device:TPU:0, one launch (start us, length us, event | category | flops | bytes accessed | tf_op | source)
XLA Modules:
  0.0 359.9 jit_solution(3037412914309126200)
XLA Ops:
  6.5 0.0 copy-start
  6.5 0.0 all-gather.2.cloned.1.call-start
  6.5 0.7 all-gather.2.cloned.1.call-update
  7.3 0.0 all-reduce.4.cloned.1.call-start
  7.3 0.7 iota_add_fusion
  8.1 0.1 broadcast_compare_fusion
  8.2 44.9 %all-gather.2.cloned.1.call-done = bf16[16,2,128,576]{3,2,1,0:T(8,128)(2,1)} async-done(((bf16[16,2,16,576]{3,2,1,0:T(8,128)(2,1)}), bf16[16,2,128,576]{3,2,1,0:T(8,128)(2,1)}) %all-gather.2.cloned.1.call-update) | async-done | bytes 4718608 | tf_op jit(solution)/shard_map/all_gather | solution.py:32
  53.0 12.0 %fusion.5 = (f32[16,2,128]{2,1,0:T(2,128)S(1)}, f32[16,2,128,512]{3,2,1,0:T(8,128)}) fusion(pred[16,2,512]{2,1,0:T(4,128)(4,1)S(1)} %broadcast_compare_fusion, bf16[16,2,128,576]{3,2,1,0:T(8,128)(2,1)} %all-gather.2.cloned.1.call-done, bf16[16,512,576]{1,2,0:T(8,128)(2,1)} %param.13), kind=kOutput, calls=%fused_computation.9 | convolution fusion | flops 2422206464 | bytes 22577152 | tf_op jit(solution)/shard_map/rjhd,rtd->rjht/dot_general | solution.py:34
  65.0 26.4 %pmax.7 = f32[16,2,128]{2,1,0:T(2,128)S(1)} all-reduce(f32[16,2,128]{2,1,0:T(2,128)S(1)} %get-tuple-element.12), channel_id=1, replica_groups=mesh['ctx'=2,'exp'=4,'req'=4] {'ctx','exp'}, use_global_device_ids=true, to_apply=%region_1.2 | all-reduce | flops 4096 | bytes 32768 | tf_op jit(solution)/shard_map/pmax | solution.py:41
  91.4 11.7 %fusion.2 = f32[16,2,128,512]{3,2,1,0:T(8,128)} fusion(bf16[16,512,576]{1,2,0:T(8,128)(2,1)} %param.13, f32[16,2,128,512]{3,2,1,0:T(8,128)} %get-tuple-element.13, f32[16,2,128]{2,1,0:T(2,128)S(1)} %pmax.7, pred[16,2,512]{2,1,0:T(4,128)(4,1)S(1)} %broadcast_compare_fusion), kind=kOutput, calls=%fused_computation.2 | convolution fusion | flops 2157969408 | bytes 25198592 | tf_op jit(solution)/shard_map/rjht,rtl->rjhl/dot_general | solution.py:45
  103.1 0.0 all-reduce.4.cloned.1.call-update
  103.1 0.0 all-reduce.6.cloned.1.call-start
  103.2 4.9 %fusion.11 = f32[16,2,128]{2,1,0:T(2,128)S(1)} fusion(f32[16,2,128,512]{3,2,1,0:T(8,128)} %get-tuple-element.13, f32[16,2,128]{2,1,0:T(2,128)S(1)} %pmax.7, pred[16,2,512]{2,1,0:T(4,128)(4,1)S(1)} %broadcast_compare_fusion), kind=kLoop, calls=%fused_computation.15 | loop fusion | flops 10481664 | bytes 8437760 | tf_op jit(solution)/shard_map/reduce_sum | solution.py:43
  108.1 27.5 %psum.29 = f32[16,2,128]{2,1,0:T(2,128)S(1)} all-reduce(f32[16,2,128]{2,1,0:T(2,128)S(1)} %fusion.11), channel_id=1, replica_groups=mesh['ctx'=2,'exp'=4,'req'=4] {'ctx','exp'}, use_global_device_ids=true, to_apply=%region_4.5 | all-reduce | flops 4096 | bytes 32768 | tf_op jit(solution)/shard_map/psum | solution.py:48
  135.6 0.1 constant_dynamic-slice_fusion
  135.7 96.1 %all-reduce.4.cloned.1.call-done = f32[16,2,128,512]{3,2,1,0:T(8,128)} async-done(((f32[16,2,128,512]{3,2,1,0:T(8,128)}), f32[16,2,128,512]{3,2,1,0:T(8,128)}) %all-reduce.4.cloned.1.call-update) | async-done | bytes 8388624 | tf_op jit(solution)/shard_map/psum | solution.py:48
  231.8 1.4 divide_convert_fusion
  233.2 0.0 copy-done
  233.2 0.6 fusion.26
  233.8 0.1 copy.25
  233.9 0.0 copy-start.3
  233.9 0.0 copy-start.4
  233.9 0.0 copy-start.1
  233.9 0.0 copy-start.2
  233.9 13.0 %fusion.41 = f32[32,7168]{1,0:T(8,128)} fusion(bf16[2048,7168]{1,0:T(8,128)(2,1)} %param.16, bf16[4,8,16,128]{3,2,1,0:T(8,128)(2,1)S(1)} %bitcast.61), kind=kOutput, calls=%fused_computation.40 | convolution fusion | flops 939524096 | bytes 30408704 | tf_op jit(solution)/shard_map/dot_general | solution.py:60
  247.0 0.0 all-reduce.6.cloned.1.call-update
  247.0 0.0 all-reduce.8.cloned.1.call-start
  247.0 0.0 copy-done.3
  247.1 0.0 copy-done.4
  247.1 0.2 reduce_window_sum.11
  247.3 56.0 %all-reduce.6.cloned.1.call-done = f32[32,7168]{1,0:T(8,128)} async-done(((f32[32,7168]{1,0:T(8,128)}), f32[32,7168]{1,0:T(8,128)}) %all-reduce.6.cloned.1.call-update) | async-done | bytes 917520 | tf_op jit(solution)/shard_map/psum | solution.py:59
  303.3 0.0 copy-done.1
  303.3 1.1 multiply_reduce_fusion
  304.4 0.0 copy-done.2
  304.4 0.2 fusion.37
  304.8 0.3 convolution_convert_fusion
  305.0 0.1 reshape.92
  305.1 8.0 %all_to_all.10 = bf16[4,4,7168]{2,1,0:T(4,128)(2,1)S(1)} all-to-all(bf16[4,4,7168]{2,1,0:T(4,128)(2,1)S(1)} %reshape.92), channel_id=1, replica_groups=mesh['ctx'=2,'exp'=4,'req'=4] {'exp'}, dimensions={0} | all-to-all | bytes 458752 | tf_op jit(solution)/shard_map/all_to_all | solution.py:92
  313.1 4.2 %fusion.9 = f32[4,4,512]{2,1,0:T(4,128)S(1)} fusion(bf16[4,4,7168]{2,1,0:T(4,128)(2,1)S(1)} %all_to_all.10, bf16[1,7168,512]{2,1,0:T(8,128)(2,1)} %param.21), kind=kOutput, calls=%fused_computation.13 | convolution fusion | flops 117440512 | bytes 7602176 | tf_op jit(solution)/shard_map/scd,df->scf/dot_general | solution.py:93
  317.4 8.1 %convolution_convert_fusion.1 = bf16[4,4,7168]{2,1,0:T(4,128)(2,1)} fusion(bf16[1,512,7168]{2,1,0:T(8,128)(2,1)} %param.23, bf16[4,4,7168]{2,1,0:T(4,128)(2,1)S(1)} %all_to_all.10, bf16[1,7168,512]{2,1,0:T(8,128)(2,1)} %param.22, f32[4,4,512]{2,1,0:T(4,128)S(1)} %fusion.9), kind=kOutput, calls=%fused_computation.8 | convolution fusion | flops 235044864 | bytes 15171584 | tf_op jit(solution)/shard_map/scf,fd->scd/dot_general | solution.py:98
  325.4 0.0 all-reduce.8.cloned.1.call-update
  325.4 17.5 %all-reduce.8.cloned.1.call-done = bf16[4,4,7168]{2,1,0:T(4,128)(2,1)} async-done(((bf16[4,4,7168]{2,1,0:T(4,128)(2,1)}), bf16[4,4,7168]{2,1,0:T(4,128)(2,1)}) %all-reduce.8.cloned.1.call-update) | async-done | bytes 229392 | tf_op jit(solution)/shard_map/psum | solution.py:104
  342.9 3.9 %all-to-all-start.1 = ((bf16[4,4,7168]{2,1,0:T(4,128)(2,1)}), bf16[4,4,7168]{2,1,0:T(4,128)(2,1)S(1)}, u32[]{:S(2)}, u32[]{:S(2)}) async-start(bf16[4,4,7168]{2,1,0:T(4,128)(2,1)} %all-reduce.8.cloned.1.call-done), calls=%async_computation.1 | async-start | bytes 458752 | tf_op jit(solution)/shard_map/all_to_all | solution.py:105
  346.8 5.6 %all-to-all-done.1 = bf16[4,4,7168]{2,1,0:T(4,128)(2,1)S(1)} async-done(((bf16[4,4,7168]{2,1,0:T(4,128)(2,1)}), bf16[4,4,7168]{2,1,0:T(4,128)(2,1)S(1)}, u32[]{:S(2)}, u32[]{:S(2)}) %all-to-all-start.1) | async-done | bytes 229408 | tf_op jit(solution)/shard_map/all_to_all | solution.py:105
  352.4 0.9 fusion.14
  (9 shorter events, 0.1 us)
Async XLA Ops:
  6.5 226.7 %copy-start = (bf16[16,512,128]{2,1,0:T(8,128)(2,1)S(1)}, bf16[16,512,128]{2,1,0:T(8,128)(2,1)}, u32[]{:S(2)}) copy-start(bf16[16,512,128]{2,1,0:T(8,128)(2,1)} %param.15) | copy-start | bytes 6291460
  6.5 46.5 %all-gather.2.cloned.1.call-start = ((), (), s32[]{:S(2)}) async-start(), calls=%async_computation.2 | async-start | bytes 5898240 | tf_op jit(solution)/shard_map/all_gather | solution.py:32
  7.3 224.6 %all-reduce.4.cloned.1.call-start = ((), (), s32[]{:S(2)}) async-start(), calls=%async_computation.3 | async-start | bytes 16777216 | tf_op jit(solution)/shard_map/psum | solution.py:48
  103.1 200.1 %all-reduce.6.cloned.1.call-start = ((), (), s32[]{:S(2)}) async-start(), calls=%async_computation.4 | async-start | bytes 1835008 | tf_op jit(solution)/shard_map/psum | solution.py:59
  233.9 13.1 %copy-start.3 = (bf16[7168]{0:T(1024)(128)(2,1)S(1)}, bf16[7168]{0:T(1024)(128)(2,1)}, u32[]{:S(2)}) copy-start(bf16[7168]{0:T(1024)(128)(2,1)} %param.18) | copy-start | bytes 43012
  233.9 13.1 %copy-start.4 = (s32[8,2]{0,1:T(2,128)S(1)}, s32[8,2]{0,1:T(2,128)}, u32[]{:S(2)}) copy-start(s32[8,2]{0,1:T(2,128)} %param.20) | copy-start | bytes 196
  233.9 69.4 %copy-start.1 = (bf16[8,7168]{1,0:T(8,128)(2,1)S(1)}, bf16[8,7168]{1,0:T(8,128)(2,1)}, u32[]{:S(2)}) copy-start(bf16[8,7168]{1,0:T(8,128)(2,1)} %param.17) | copy-start | bytes 344068
  233.9 70.5 %copy-start.2 = (bf16[7168,4]{0,1:T(4,128)(2,1)S(1)}, bf16[7168,4]{0,1:T(4,128)(2,1)}, u32[]{:S(2)}) copy-start(bf16[7168,4]{0,1:T(4,128)(2,1)} %param.19) | copy-start | bytes 172036
  247.0 96.0 %all-reduce.8.cloned.1.call-start = ((), (), s32[]{:S(2)}) async-start(), calls=%async_computation.5 | async-start | bytes 458752 | tf_op jit(solution)/shard_map/psum | solution.py:104
  342.9 9.5 %all-to-all-start.1 = ((bf16[4,4,7168]{2,1,0:T(4,128)(2,1)}), bf16[4,4,7168]{2,1,0:T(4,128)(2,1)S(1)}, u32[]{:S(2)}, u32[]{:S(2)}) async-start(bf16[4,4,7168]{2,1,0:T(4,128)(2,1)} %all-reduce.8.cloned.1.call-done), calls=%async_computation.1 | async-start | bytes 458752 | tf_op jit(solution)/shard_map/all_to_all | solution.py:105
Sparse Core Ops, SparseCore 0:
  9.3 43.7 all-gather.1
  103.3 128.5 all-reduce.3
  247.1 56.1 all-reduce.5
  325.6 17.3 all-reduce.7
where the time goes:
time: 360 us
  waiting for transfers between devices  221 us (61%)
  blocking collectives  62 us (17%)
  matrix products  50.9 us (14%)
  between operations  13.3 us (4%)
  other arithmetic  8.52 us (2%)
  starting transfers between devices  4.03 us (1%)
    psum x1, waiting for transfers between devices, on_device(): summed, sum_all = lax.psum((weighted, weight_sum), ('ctx', 'exp'))  96.1 us
    psum x1, waiting for transfers between devices, on_device(): lax.psum(jnp.dot(head_out, out_proj, preferred_element_type=jnp.float32),...  56 us
    all_gather x1, waiting for transfers between devices, on_device(): all_queries = lax.all_gather(queries, ('ctx', 'exp'), axis=2, tiled=True)  44.9 us
    psum x1, blocking collectives, on_device(): summed, sum_all = lax.psum((weighted, weight_sum), ('ctx', 'exp'))  27.5 us
    pmax x1, blocking collectives, on_device(): row_max = lax.pmax(jnp.max(masked, axis=-1), ('ctx', 'exp'))  26.4 us
    psum x1, waiting for transfers between devices, on_device(): lax.psum(partial_out.astype(jnp.bfloat16), 'ctx').astype(jnp.float32)  17.5 us
    dot_general x1, matrix products, on_device(): jnp.dot(head_out, out_proj, preferred_element_type=jnp.float32)  13 us
    dot_general x1, matrix products, on_device(): jnp.einsum('rjhd,rtd->rjht', all_queries, latent_cache, preferred_element...  12 us
  transfers between devices with their start and end apart: 5, of which 5 were waited for; matrix products, arithmetic and copies ran while one was open for 2% of the time, Pallas kernels for 0%

commit v1 on v0

--- a/solution.py
+++ b/solution.py
@@ -1,8 +1,11 @@
+import functools
 import math
 
 import jax
 import jax.numpy as jnp
 from jax import lax
+from jax.experimental import pallas as pl
+from jax.experimental.pallas import tpu as pltpu
 from jax.sharding import PartitionSpec as P
 
 route_scale = 2.5
@@ -114,9 +117,480 @@
     return (own_cols + mixture).astype(jnp.bfloat16)
 
 
+MESH = pl.DeviceIdType.MESH
+F32 = jnp.float32
+BF16 = jnp.bfloat16
+PAIR = 2
+SLOTS = 5
+BLOCKS = 8
+AHEAD = 3
+
+
+def lay_out(chunks):
+    places, count = {}, 0
+    for name, number in (
+        ("own", 3), ("diag", 2), ("core", 4), ("stat", 7), ("fold", 1), ("cross", 2), ("last", 2),
+    ):
+        places[name] = (count, number)
+        count += number * chunks
+    for name, number in (("route", 3), ("swap", 2), ("rows", 6), ("hid", 4), ("hidfwd", 3)):
+        places[name] = (count, number)
+        count += number
+    return places, count
+
+
+def contract(a, b, da, db):
+    return lax.dot_general(a, b, (((da,), (db,)), ((), ())), preferred_element_type=F32)
+
+
+def layer_kernel(
+    lens, q_hbm, cache_hbm, vu_hbm, op_hbm, res, gain, router_hbm, routes, eg_hbm, eu_hbm, ed_hbm,
+    out,
+    qbuf, cbuf, acc, mown, stat, norm, crx, x2, y2, x3, y3, ctx2, vu, ho, wslot, eg, eu, router,
+    chosen, pbuf, prx, tsum, rrx, hid, xn, act, gcol,
+    send, recv, csem, wsem, osem,
+):
+    chunks, _, heads_rows, width = q_hbm.shape
+    heads = heads_rows // 2
+    block_len, latent = cache_hbm.shape[2], vu.shape[1]
+    vdim = vu.shape[2]
+    places, _ = lay_out(chunks)
+    scale = 1.0 / math.sqrt(vdim + width - latent)
+    half = hid.shape[3]
+    cols = half * 2 // BLOCKS
+    per_half = BLOCKS // 2
+    c = lax.axis_index("ctx")
+    e = lax.axis_index("exp")
+    ey, ex = e // 2, e % 2
+    me = c * 4 + e
+    ex_n = e + 1 - 2 * ex
+    ey_n = e + 2 - 4 * ey
+    ed_n = 3 - e
+    others = (ex_n, ey_n, ed_n)
+    peers = [(1 - c, e)] + [(c, o) for o in others] + [(1 - c, o) for o in others]
+
+    def remote(kind, g, k, src, dst, to):
+        first, stride = places[kind]
+        place = first + g * stride + k
+        return pltpu.make_async_remote_copy(
+            src_ref=src, dst_ref=dst, send_sem=send.at[place], recv_sem=recv.at[place],
+            device_id={"ctx": to[0], "exp": to[1]}, device_id_type=MESH,
+        )
+
+    core_to, x_to, y_to = (1 - c, e), (c, ex_n), (c, ey_n)
+
+    def own_copy(g, k):
+        return remote("own", g, k, q_hbm.at[g], qbuf.at[g, me], (core_to, x_to, y_to)[k])
+
+    def diag_copy(g, k):
+        source = c * 4 + (ex_n if k == 0 else ey_n)
+        view = qbuf.at[g, source, k]
+        return remote("diag", g, k, view, view, (y_to, x_to)[k])
+
+    def core_copy(g, k):
+        source = c * 4 + (ex_n, ey_n, ed_n, ed_n)[k]
+        view = qbuf.at[g, source] if k < 2 else qbuf.at[g, source, k - 2]
+        return remote("core", g, k, view, view, core_to)
+
+    def stat_copy(g, k):
+        return remote("stat", g, k, stat.at[g, me], stat.at[g, me], peers[k])
+
+    def fold_copy(g):
+        return remote("fold", g, 0, norm.at[g, 1 - c], crx.at[g], core_to)
+
+    def cross_copy(g, k):
+        if k == 0:
+            return remote("cross", g, 0, crx.at[g, :, 1 - ex, 0], x2.at[g], x_to)
+        return remote("cross", g, 1, crx.at[g, 1 - ey, :, 1], y2.at[g], y_to)
+
+    def last_copy(g, k):
+        if k == 0:
+            return remote("last", g, 0, x2.at[g, 1 - ey], y3.at[g], y_to)
+        return remote("last", g, 1, y2.at[g, 1 - ex], x3.at[g], x_to)
+
+    def route_copy(k):
+        return remote("route", 0, k, chosen.at[e], chosen.at[e], (c, others[k]))
+
+    def swap_copy(p):
+        return remote("swap", 0, p, pbuf.at[p, 0], prx.at[p], core_to)
+
+    def rows_copy(p, k):
+        return remote("rows", 0, p * 3 + k, tsum.at[p, others[k]], rrx.at[p, k], (c, others[k]))
+
+    def hid_copy(k):
+        to = (x_to, y_to, (c, ed_n), core_to)[k]
+        return remote("hid", 0, k, hid.at[e, c], hid.at[e, c], to)
+
+    def hidfwd_copy(k):
+        view = hid.at[others[k], c]
+        return remote("hidfwd", 0, k, view, view, core_to)
+
+    def cache_copy(g):
+        return pltpu.make_async_copy(cache_hbm.at[g], cbuf.at[g % 2], csem.at[g % 2])
+
+    def column(i):
+        side = jnp.where(i < per_half, 1 - c, c)
+        return pl.multiple_of((side * per_half + i % per_half) * cols, cols)
+
+    def op_copy(i):
+        return pltpu.make_async_copy(
+            op_hbm.at[:, pl.ds(column(i), cols)], wslot.at[i % SLOTS], osem.at[i % SLOTS]
+        )
+
+    depth = ed_hbm.shape[0]
+
+    def down_copy(i):
+        place = pl.ds(pl.multiple_of((i % 4) * depth, depth), depth)
+        return pltpu.make_async_copy(
+            ed_hbm.at[:, pl.ds(column(i), cols)], wslot.at[3 + i // 4, place], wsem.at[4 + i]
+        )
+
+    own_q = pltpu.make_async_copy(q_hbm, qbuf.at[:, me], wsem.at[0])
+    vu_copy = pltpu.make_async_copy(vu_hbm, vu, wsem.at[1])
+    eg_copy = pltpu.make_async_copy(eg_hbm, eg, wsem.at[2])
+    eu_copy = pltpu.make_async_copy(eu_hbm, eu, wsem.at[3])
+    router_copy = pltpu.make_async_copy(router_hbm, router, wsem.at[4 + BLOCKS])
+
+    own_q.start()
+    cache_copy(0).start()
+    lanes = lax.broadcasted_iota(jnp.int32, chosen.shape[1:], 1)
+    named = (routes[:, 0:1] == lanes) | (routes[:, 1:2] == lanes)
+    chosen[e] = named.astype(F32)
+
+    barrier = pltpu.get_barrier_semaphore()
+    for to in peers:
+        pl.semaphore_signal(
+            barrier, inc=1, device_id={"ctx": to[0], "exp": to[1]}, device_id_type=MESH
+        )
+    pl.semaphore_wait(barrier, len(peers))
+
+    for g in range(AHEAD):
+        for k in range(3):
+            own_copy(g, k).start()
+    for k in range(3):
+        route_copy(k).start()
+    vu_copy.start()
+    router_copy.start()
+    own_q.wait()
+
+    rows = 8 * heads_rows
+
+    def attend(g):
+        cache_copy(g).wait()
+
+        @pl.when(g + 1 < chunks)
+        def _():
+            cache_copy(g + 1).start()
+
+        for r in range(PAIR):
+            q = qbuf[g, :, r].reshape(rows, width)
+            keys = cbuf[g % 2, r]
+            s = contract(keys, q, 1, 1) * scale
+            position = me * block_len + lax.broadcasted_iota(jnp.int32, s.shape, 0)
+            later = lax.broadcasted_iota(jnp.int32, s.shape, 1) // heads % 2
+            visible = position < lens[g * PAIR + r] + later
+            s = jnp.where(visible, s, -1e30)
+            m = jnp.max(s, axis=0, keepdims=True)
+            p = jnp.where(visible, jnp.exp(s - m), 0.0)
+            total = jnp.sum(p, axis=0, keepdims=True)
+            acc[g % 2, r] = contract(p.astype(BF16), keys[:, :latent], 0, 0)
+            mown[g % 2, r : r + 1] = m
+            z = jnp.where(total > 0.0, m + jnp.log(jnp.maximum(total, 1e-30)), -1e30)
+            stat[g, me, r : r + 1] = z
+        for k in range(7):
+            stat_copy(g, k).start()
+
+    def normalise(g):
+        for k in range(7):
+            stat_copy(g, k).wait_recv()
+        for r in range(PAIR):
+            z = stat[g, :, r]
+            top = jnp.max(z, axis=0, keepdims=True)
+            whole = top + jnp.log(jnp.sum(jnp.exp(z - top), axis=0, keepdims=True))
+            factor = jnp.exp(mown[g % 2, r : r + 1] - whole)
+            factor = jnp.transpose(jnp.broadcast_to(factor, (128, rows)))
+            for k in range(latent // 128):
+                part = acc[g % 2, r, :, k * 128 : (k + 1) * 128] * factor
+                norm[g, :, :, :, r, :, k * 128 : (k + 1) * 128] = part.astype(BF16).reshape(
+                    2, 2, 2, heads_rows, 128
+                )
+        fold_copy(g).start()
+
+    def fold(g):
+        fold_copy(g).wait_recv()
+        crx[g] = (crx[g].astype(F32) + norm[g, c].astype(F32)).astype(BF16)
+        cross_copy(g, 0).start()
+        cross_copy(g, 1).start()
+
+    def cross(g):
+        cross_copy(g, 0).wait_recv()
+        x2[g] = (x2[g].astype(F32) + crx[g, :, ex, 0].astype(F32)).astype(BF16)
+        last_copy(g, 0).start()
+        cross_copy(g, 1).wait_recv()
+        y2[g] = (y2[g].astype(F32) + crx[g, ey, :, 1].astype(F32)).astype(BF16)
+        last_copy(g, 1).start()
+
+    def last(g):
+        last_copy(g, 0).wait_recv()
+        ctx2[g % 2, 0] = (x2[g, ey].astype(F32) + y3[g].astype(F32)).astype(BF16)
+        last_copy(g, 1).wait_recv()
+        ctx2[g % 2, 1] = (y2[g, ex].astype(F32) + x3[g].astype(F32)).astype(BF16)
+
+        @pl.when(g % 2 == 1)
+        def _():
+            both = ctx2[...].reshape(4 * heads_rows, latent)
+            for h in range(heads):
+                every = jnp.dot(both, vu[h], preferred_element_type=F32).reshape(8, heads, vdim)
+                mine = lax.broadcasted_iota(jnp.int32, every.shape, 1) == h
+                place = pl.ds(pl.multiple_of((g // 2) * 8, 8), 8)
+                ho[place, h * vdim : (h + 1) * vdim] = jnp.sum(
+                    jnp.where(mine, every, 0.0), axis=1
+                )
+
+    vu_copy.wait()
+
+    def step(s, _):
+        def at(lag, run):
+            @pl.when((s >= lag) & (s < chunks + lag))
+            def _():
+                run(s - lag)
+
+        @pl.when(s + AHEAD < chunks)
+        def _():
+            for k in range(3):
+                own_copy(s + AHEAD, k).start()
+
+        def forward(g):
+            own_copy(g, 1).wait_recv()
+            diag_copy(g, 0).start()
+            core_copy(g, 0).start()
+            own_copy(g, 2).wait_recv()
+            diag_copy(g, 1).start()
+            core_copy(g, 1).start()
+
+        def forward_diag(g):
+            for k in range(2):
+                diag_copy(g, k).wait_recv()
+                core_copy(g, 2 + k).start()
+
+        def attend_when_here(g):
+            own_copy(g, 0).wait_recv()
+            for k in range(4):
+                core_copy(g, k).wait_recv()
+            attend(g)
+
+        at(0, forward)
+        at(1, forward_diag)
+        at(3, normalise)
+        at(4, fold)
+        at(5, cross)
+        at(6, last)
+        at(2, attend_when_here)
+
+        @pl.when(s < SLOTS)
+        def _():
+            op_copy(s).start()
+
+        @pl.when(s == SLOTS)
+        def _():
+            eg_copy.start()
+
+        @pl.when(s == SLOTS + 1)
+        def _():
+            eu_copy.start()
+
+        return 0
+
+    lax.fori_loop(0, chunks + 6, step, 0)
+
+    own_rows = res.shape[0]
+
+    def project(i, _):
+        op_copy(i).wait()
+        part = jnp.dot(ho[...].astype(BF16), wslot[i % SLOTS], preferred_element_type=F32)
+        place = pl.ds(pl.multiple_of((i % per_half) * cols, cols), cols)
+        pbuf[0, i // per_half, :, :, place] = part.astype(BF16).reshape(4, own_rows, cols)
+
+        @pl.when(i + SLOTS < BLOCKS)
+        def _():
+            op_copy(i + SLOTS).start()
+
+        @pl.when(i == per_half - 1)
+        def _():
+            swap_copy(0).start()
+
+        return 0
+
+    lax.fori_loop(0, BLOCKS, project, 0)
+    for i in range(BLOCKS):
+        down_copy(i).start()
+
+    def reduce_rows(p):
+        swap_copy(p).wait_recv()
+        tsum[p] = (prx[p].astype(F32) + pbuf[p, 1].astype(F32)).astype(BF16)
+        for k in (2, 0, 1):
+            rows_copy(p, k).start()
+        total = tsum[p, e].astype(F32)
+        for k in range(3):
+            rows_copy(p, k).wait_recv()
+            total = total + rrx[p, k].astype(F32)
+        return total
+
+    own_cols = pl.ds(pl.multiple_of(c * half, half), half)
+    hid[e, c] = (res[:, own_cols].astype(F32) + reduce_rows(0)).astype(BF16)
+    for k in (2, 0, 1, 3):
+        hid_copy(k).start()
+    for k in range(3):
+        hid_copy(k).wait_recv()
+        hidfwd_copy(k).start()
+    hid_copy(3).wait_recv()
+    for k in range(3):
+        hidfwd_copy(k).wait_recv()
+        route_copy(k).wait_recv()
+    router_copy.wait()
+    eg_copy.wait()
+    eu_copy.wait()
+
+    sides = [hid[:, side].astype(F32).reshape(4 * own_rows, half) for side in range(2)]
+    squares = sum(jnp.sum(v * v, axis=-1, keepdims=True) for v in sides)
+    inverse = lax.rsqrt(squares / (2 * half) + 1e-06)
+    for side in range(2):
+        spread = gain[:, side * half : (side + 1) * half].astype(F32)
+        xn[side] = (sides[side] * inverse * spread).astype(BF16)
+    span = [slice(side * half, (side + 1) * half) for side in range(2)]
+    both_sides = lambda w: sum(
+        jnp.dot(xn[side], w[span[side], :], preferred_element_type=F32) for side in range(2)
+    )
+    affinity = jax.nn.sigmoid(both_sides(router))
+    picked = affinity * chosen[...].reshape(4 * own_rows, 128)[:, : affinity.shape[1]]
+    weights = route_scale * picked / jnp.sum(picked, axis=-1, keepdims=True)
+    mine = lax.broadcasted_iota(jnp.int32, weights.shape, 1) == e
+    gcol[...] = jnp.broadcast_to(
+        jnp.sum(jnp.where(mine, weights, 0.0), axis=-1, keepdims=True), gcol.shape
+    )
+    gate_part = both_sides(eg)
+    up_part = both_sides(eu)
+    act[...] = (gate_part / (1.0 + jnp.exp(-gate_part)) * up_part).astype(BF16)
+
+    for i in range(BLOCKS):
+        down_copy(i).wait()
+        block = wslot[3 + i // 4, (i % 4) * depth : (i % 4 + 1) * depth]
+        part = jnp.dot(act[...], block, preferred_element_type=F32) * gcol[:, 0:1]
+        place = slice((i % per_half) * cols, (i % per_half + 1) * cols)
+        pbuf[1, i // per_half, :, :, place] = part.astype(BF16).reshape(4, own_rows, cols)
+        if i == per_half - 1:
+            swap_copy(1).start()
+    out[...] = (hid[e, c].astype(F32) + reduce_rows(1)).astype(BF16)
+
+    def drain(g, _):
+        for k in range(3):
+            own_copy(g, k).wait_send()
+        for k in range(2):
+            diag_copy(g, k).wait_send()
+            cross_copy(g, k).wait_send()
+            last_copy(g, k).wait_send()
+        for k in range(4):
+            core_copy(g, k).wait_send()
+        for k in range(7):
+            stat_copy(g, k).wait_send()
+        fold_copy(g).wait_send()
+        return 0
+
+    lax.fori_loop(0, chunks, drain, 0)
+    for k in range(3):
+        route_copy(k).wait_send()
+        hidfwd_copy(k).wait_send()
+        rows_copy(0, k).wait_send()
+        rows_copy(1, k).wait_send()
+    for k in range(4):
+        hid_copy(k).wait_send()
+    for p in range(2):
+        swap_copy(p).wait_send()
+
+
+def fused_on_device(
+    queries, latent_cache, context_lengths, value_up, out_proj, residual, norm_gain, router,
+    routes, expert_gate, expert_up, expert_down,
+):
+    reqs, verify, heads, width = queries.shape
+    chunks = reqs // PAIR
+    hr = verify * heads
+    _, block_len, _ = latent_cache.shape
+    _, latent, vdim = value_up.shape
+    own_rows, model = residual.shape
+    half = model // 2
+    ff = expert_down.shape[1]
+    rows = 8 * hr
+    _, count = lay_out(chunks)
+    vmem, anywhere = pl.BlockSpec(memory_space=pltpu.VMEM), pl.BlockSpec(memory_space=pl.ANY)
+    scratch = [
+        pltpu.VMEM((chunks, 8, PAIR, hr, width), BF16),
+        pltpu.VMEM((2, PAIR, block_len, width), BF16),
+        pltpu.VMEM((2, PAIR, rows, latent), F32),
+        pltpu.VMEM((2, PAIR, rows), F32),
+        pltpu.VMEM((chunks, 8, PAIR, rows), F32),
+        pltpu.VMEM((chunks, 2, 2, 2, PAIR, hr, latent), BF16),
+        pltpu.VMEM((chunks, 2, 2, PAIR, hr, latent), BF16),
+        pltpu.VMEM((chunks, 2, hr, latent), BF16),
+        pltpu.VMEM((chunks, 2, hr, latent), BF16),
+        pltpu.VMEM((chunks, hr, latent), BF16),
+        pltpu.VMEM((chunks, hr, latent), BF16),
+        pltpu.VMEM((2, PAIR, hr, latent), BF16),
+        pltpu.VMEM((heads, latent, vdim), BF16),
+        pltpu.VMEM((reqs * verify, heads * vdim), F32),
+        pltpu.VMEM((SLOTS, heads * vdim, model // BLOCKS), BF16),
+        pltpu.VMEM((model, ff), BF16),
+        pltpu.VMEM((model, ff), BF16),
+        pltpu.VMEM(router.shape, BF16),
+        pltpu.VMEM((4, own_rows, 128), F32),
+        pltpu.VMEM((2, 2, 4, own_rows, half), BF16),
+        pltpu.VMEM((2, 4, own_rows, half), BF16),
+        pltpu.VMEM((2, 4, own_rows, half), BF16),
+        pltpu.VMEM((2, 3, own_rows, half), BF16),
+        pltpu.VMEM((4, 2, own_rows, half), BF16),
+        pltpu.VMEM((2, 4 * own_rows, half), BF16),
+        pltpu.VMEM((4 * own_rows, ff), BF16),
+        pltpu.VMEM((4 * own_rows, 128), F32),
+        pltpu.SemaphoreType.DMA((count,)),
+        pltpu.SemaphoreType.DMA((count,)),
+        pltpu.SemaphoreType.DMA((2,)),
+        pltpu.SemaphoreType.DMA((5 + BLOCKS,)),
+        pltpu.SemaphoreType.DMA((SLOTS,)),
+    ]
+    return pl.pallas_call(
+        layer_kernel,
+        out_shape=jax.ShapeDtypeStruct((own_rows, half), BF16),
+        in_specs=[pl.BlockSpec(memory_space=pltpu.SMEM)] + [anywhere] * 4 + [vmem] * 2
+        + [anywhere, vmem] + [anywhere] * 3,
+        out_specs=vmem,
+        scratch_shapes=scratch,
+        compiler_params=pltpu.CompilerParams(
+            collective_id=0, has_side_effects=True, vmem_limit_bytes=62 * 1024 * 1024
+        ),
+        cost_estimate=pl.CostEstimate(
+            flops=6_000_000_000, bytes_accessed=64_000_000, transcendentals=2_000_000
+        ),
+    )(
+        context_lengths,
+        queries.reshape(chunks, PAIR, hr, width),
+        latent_cache.reshape(chunks, PAIR, block_len, width),
+        value_up,
+        out_proj,
+        residual,
+        norm_gain.reshape(1, model),
+        router,
+        routes,
+        expert_gate[0],
+        expert_up[0],
+        expert_down[0],
+    )
+
+
 def solution(mesh):
+    grouped = mesh.shape["ctx"] == 2 and mesh.shape["exp"] == 4
+    body = fused_on_device if grouped else on_device
     return jax.shard_map(
-        on_device,
+        body,
         mesh=mesh,
         in_specs=(
             P("req", None, ("ctx", "exp"), None),

time: 360 us -> 123 us (0.34)
  waiting for transfers between devices: 221 us -> 0 us
  Pallas kernels: 0 us -> 102 us
  blocking collectives: 62 us -> 0 us
  matrix products: 50.9 us -> 0 us
  local copies, waits for them, and re-layouts: 0.25 us -> 20.7 us
  between operations: 13.3 us -> 0.01 us
  other arithmetic: 8.52 us -> 0 us
  starting transfers between devices: 4.03 us -> 0 us
    psum x3 -> x0, waiting for transfers between devices: 170 us -> none  [the longest x1 96.1 us: on_device(): summed, sum_all = lax.psum((weighted, weight_sum), ('ctx', 'exp'))]
    pallas_call x0 -> x1, Pallas kernels: none -> 102 us  [fused_on_device(): pl.pallas_call(layer_kernel, out_shape=jax.ShapeDtypeStruct((own_rows, ha...]
    dot_general x9 -> x0, matrix products: 50.9 us -> none  [the longest x1 13 us: on_device(): jnp.dot(head_out, out_proj, preferred_element_type=jnp.float32)]
    all_gather x1 -> x0, waiting for transfers between devices: 44.9 us -> none  [on_device(): all_queries = lax.all_gather(queries, ('ctx', 'exp'), axis=2, tiled=True)]
    psum x1 -> x0, blocking collectives: 27.5 us -> none  [on_device(): summed, sum_all = lax.psum((weighted, weight_sum), ('ctx', 'exp'))]
    pmax x1 -> x0, blocking collectives: 26.4 us -> none  [on_device(): row_max = lax.pmax(jnp.max(masked, axis=-1), ('ctx', 'exp'))]
    unnamed x10 -> x4, local copies, waits for them, and re-layouts: 0.03 us -> 19.3 us
    all_to_all x1 -> x0, blocking collectives: 8.01 us -> none  [on_device(): lax.all_to_all(outgoing, 'exp', split_axis=0, concat_axis=0, tiled=True)]
  transfers between devices with their start and end apart: 5 -> 0, of which waited for: 5 -> 0; matrix products, arithmetic and copies ran while one was open for 2% -> 0% of each run, Pallas kernels for 0% -> 0%
where the time goes in v1:
time: 123 us; the launch traced here: 122 us
  Pallas kernels  102 us (83%)
  local copies, waits for them, and re-layouts  20.7 us (17%)
    pallas_call x1, Pallas kernels, fused_on_device(): pl.pallas_call(layer_kernel, out_shape=jax.ShapeDtypeStruct((own_rows, ha...  102 us
    unnamed x4, local copies, waits for them, and re-layouts  19.3 us

profile of v1, /device:TPU:0, one launch (start us, length us, event | category | flops | bytes accessed | tf_op | source)
XLA Modules:
  0.0 122.5 jit_solution(18326698147080315067)
XLA Ops:
  0.0 1.3 %copy.15.routes = s32[8,2]{1,0:T(8,128)} copy(s32[8,2]{0,1:T(2,128)} %param.20) | data formatting | bytes 128 | tf_op args[8]
  1.3 1.3 %reshape.11.gain = bf16[1,7168]{1,0:T(2,128)(2,1)} reshape(bf16[7168]{0:T(1024)(128)(2,1)} %param.18) | data formatting | bytes 28672 | tf_op jit(solution)/shard_map/reshape | solution.py:580
  2.7 2.4 %copy.14.router_hbm = bf16[7168,4]{1,0:T(8,128)(2,1)} copy(bf16[7168,4]{0,1:T(4,128)(2,1)} %param.19) | data formatting | bytes 114688 | tf_op args[7]
  5.1 14.1 %copy.13 = bf16[16,512,576]{2,1,0:T(8,128)(2,1)} copy(bf16[16,512,576]{1,2,0:T(8,128)(2,1)} %param.13) | data formatting | bytes 18874368 | tf_op args[1]
  19.2 101.8 %shard_map.118 = bf16[8,3584]{1,0:T(8,128)(2,1)} custom-call(s32[16]{0:T(128)} %lens.1, bf16[8,2,32,576]{3,2,1,0:T(8,128)(2,1)} %bitcast.9, bf16[8,2,512,576]{3,2,1,0:T(8,128)(2,1)} %bitcast.5, bf16[16,512,128]{2,1,0:T(8,128)(2,1)} %vu_hbm.1, bf16[2048,7168]{1,0:T(8,128)(2,1)} %op_hbm.1, bf16[8,7168]{1,0:T(8,128)(2,1)} %res.1, ...), custom_call_target="tpu_custom_call" | custom-call | flops 6000000000 | bytes 64000000 | tf_op jit(solution)/shard_map/pallas_call | solution.py:560
  121.0 1.4 %copy.17 = bf16[8,3584]{1,0:T(8,128)(2,1)} copy(bf16[8,3584]{1,0:T(8,128)(2,1)} %shard_map.118) | data formatting | bytes 114688
